TPU v7x, 32 devices: a whole 2x2x4 slice. The times are simulated.
32 devices in a mesh: ctx: 8 (over z, x), head: 4 (over y, core).
Axes of the slice: x: 2, y: 2, z: 4, core: 2. Of those that a mesh axis runs over, the one named last changes fastest.
Arguments:
- features: bfloat16 [2048, 16384], P('ctx', 'head'), may hold values from -6 to 6
- log_decay: float32 [256, 2048], P('head', 'ctx'), may hold values from -2 to 0, as said below
- step_size: float32 [256, 2048], P('head', 'ctx'), may hold values from 0.0002 to 0.002
- b_matrix: bfloat16 [2048, 2048], P('ctx', 'head'), may hold values from -6 to 6
- c_matrix: bfloat16 [2048, 2048], P('ctx', 'head'), may hold values from -6 to 6
- skip_gain: float32 [256], P('head'), may hold values from 0.5 to 1.5
Outputs:
- mixed: bfloat16 [2048, 16384], P('ctx', 'head')
Inputs may be any that keep to these rules, and one draw needn't show every extreme that they name: `log_decay`: every entry is negative.
All inputs are finite; a program needn't handle non-finite values.
Results may differ from a plain program's by a relative error of at most 0.0013.
Values sent between devices are 32-bit elements; how exact they have to be, the bound alone decides.
A program may use at most 320 MiB of HBM per device.

v0:
```python
import functools

import jax
import jax.numpy as jnp
from jax import lax
from jax.experimental import pallas as pl
from jax.experimental.pallas import tpu as pltpu
from jax.sharding import PartitionSpec as P

N = 256
SPAN = 128
UNIT = 8
MESH = pl.DeviceIdType.MESH
LIMIT = 56 * 1024 * 1024
BF = jnp.bfloat16
F32 = jnp.float32


def scale_kernel(width, x_ref, co_ref, wt_ref):
    for h in range(UNIT):
        cols = slice(h * width, (h + 1) * width)
        wt_ref[:, cols] = (x_ref[:, cols].astype(F32) * co_ref[0, :, h : h + 1]).astype(BF).astype(F32)


def mix_kernel(width, x_ref, ct_ref, cr_ref, st_ref, b_ref, c_ref, skip_ref, sp_ref, o_ref):
    row = lax.broadcasted_iota(jnp.int32, (SPAN, SPAN), 0)
    col = lax.broadcasted_iota(jnp.int32, (SPAN, SPAN), 1)
    causal = row >= col
    for k in range(2):
        toks = slice(k * SPAN, (k + 1) * SPAN)
        scores = lax.dot_general(
            c_ref[toks, :], b_ref[toks, :], (((1,), (1,)), ((), ())), preferred_element_type=F32
        )
        for h in range(UNIT):
            cols = slice(h * width, (h + 1) * width)
            down = ct_ref[0, toks, h : h + 1]
            gaps = jnp.where(causal, down - cr_ref[0, h : h + 1, toks], -jnp.inf)
            weights = (scores * jnp.exp(gaps) * st_ref[0, h : h + 1, toks]).astype(BF)
            x = x_ref[toks, cols]
            part = jnp.dot(weights, x, preferred_element_type=F32)
            part = part + sp_ref[toks, cols] * jnp.exp(down)
            o_ref[toks, cols] = (part + skip_ref[:, cols] * x.astype(F32)).astype(BF)


def chain_kernel(
    n, chunk, glanes, wt, bt, cc, dec, out,
    bt_in, cc_in, dec_in, x_in, b_slot, c_slot, d_slot, states, f_out, f_in, k_out, k_in, y_out,
    small_s, small_r, x_s, x_r, f_s, f_r, k_s, k_r, yf_s, yf_r, yk_s, yk_r,
):
    me = lax.axis_index("ctx")
    level, side = me // 2, lax.rem(me, 2)
    levels = n // 2
    partner = me + 1 - 2 * side
    after, before = lax.rem(me + 2, n), lax.rem(me + n - 2, n)
    half = dec_in.shape[1]
    count = half // chunk
    groups = bt.shape[0] // N
    held = bt_in.shape[0] // N
    mine, other = side * half, (1 - side) * half
    g_mine, g_other = (side * groups) // 2 * N, ((1 - side) * groups) // 2 * N

    barrier = pltpu.get_barrier_semaphore()
    for device in (partner, after, before):
        pl.semaphore_signal(barrier, inc=1, device_id={"ctx": device}, device_id_type=MESH)
    pl.semaphore_wait(barrier, 3)

    def remote(src, dst, send, recv, device):
        return pltpu.make_async_remote_copy(
            src_ref=src, dst_ref=dst, send_sem=send, recv_sem=recv,
            device_id={"ctx": device}, device_id_type=MESH,
        )

    def at(start, length):
        return pl.ds(pl.multiple_of(start, 128), length)

    smalls = [
        remote(bt.at[at(g_other, held * N), :], bt_in, small_s.at[0], small_r.at[0], partner),
        remote(cc.at[:, at(g_other, held * N)], cc_in, small_s.at[1], small_r.at[1], partner),
        remote(dec.at[:, at(other, half)], dec_in, small_s.at[2], small_r.at[2], partner),
    ]

    def x_copy(c):
        return remote(wt.at[:, at(other + c * chunk, chunk)], x_in.at[c], x_s.at[c], x_r.at[c], partner)

    def f_copy(c):
        return remote(f_out.at[c], f_in.at[c], f_s.at[c], f_r.at[c], after)

    def k_copy(c):
        return remote(k_out.at[c], k_in.at[c], k_s.at[c], k_r.at[c], before)

    def y_copy(c, k):
        send, recv = (yf_s, yf_r) if k == 0 else (yk_s, yk_r)
        return remote(
            y_out.at[k, c], out.at[pl.ds(k * SPAN, SPAN), at(mine + c * chunk, chunk)],
            send.at[c], recv.at[c], partner,
        )

    def y_landed(c, k):
        send, recv = (yf_s, yf_r) if k == 0 else (yk_s, yk_r)
        return remote(
            y_out.at[k, c], out.at[pl.ds(k * SPAN, SPAN), at(other + c * chunk, chunk)],
            send.at[c], recv.at[c], partner,
        )

    for copy in smalls:
        copy.start()

    @pl.loop(0, count)
    def _(c):
        x_copy(c).start()

    here = (side, 3 - side)
    there = (1 - side, 2 + side)
    for k in range(2):
        toks = slice(k * SPAN, (k + 1) * SPAN)
        b_slot[here[k]] = bt[at(g_mine, held * N), toks].astype(BF)
        c_slot[here[k]] = cc[toks, at(g_mine, held * N)].astype(BF)
        d_slot[here[k]] = jnp.broadcast_to(dec[k : k + 1, at(mine, half)], (8, half))
    for copy in smalls:
        copy.wait_recv()
    for k in range(2):
        toks = slice(k * SPAN, (k + 1) * SPAN)
        b_slot[there[k]] = bt_in[:, toks].astype(BF)
        c_slot[there[k]] = cc_in[toks, :].astype(BF)
        d_slot[there[k]] = jnp.broadcast_to(dec_in[k : k + 1, :], (8, half))

    def group_rows(c):
        return at((c * chunk) // glanes * N, N)

    def outputs(c, k, slot, entering):
        y = jnp.dot(
            c_slot[slot, :, group_rows(c)], entering.astype(BF), preferred_element_type=F32
        )

        @pl.when(here[k] == slot)
        def _():
            out[pl.ds(k * SPAN, SPAN), at(mine + c * chunk, chunk)] = y

        @pl.when(here[k] != slot)
        def _():
            y_out[k, c] = y

    def advance(c, slot, entering):
        d = d_slot[slot, 0:1, at(c * chunk, chunk)]
        return d * entering + states[c, slot]

    def forward(c):
        x_copy(c).wait_recv()
        for k in range(2):
            toks = slice(k * SPAN, (k + 1) * SPAN)
            states[c, here[k]] = jnp.dot(
                b_slot[here[k], group_rows(c), :], wt[toks, at(mine + c * chunk, chunk)].astype(BF),
                preferred_element_type=F32,
            )
            states[c, there[k]] = jnp.dot(
                b_slot[there[k], group_rows(c), :], x_in[c, toks, :].astype(BF),
                preferred_element_type=F32,
            )

        @pl.when(level == 0)
        def _():
            f_in[c] = jnp.zeros(f_in.shape[1:], F32)

        @pl.when(level > 0)
        def _():
            f_copy(c).wait_recv()

        first = f_in[c]
        second = advance(c, 0, first)
        last = advance(c, 1, second)

        @pl.when(level < levels - 1)
        def _():
            f_out[c] = last
            f_copy(c).start()

        @pl.when(level == levels - 1)
        def _():
            k_in[c] = last

        outputs(c, 0, 0, first)
        outputs(c, 0, 1, second)
        y_copy(c, 0).start()

    def backward(c):
        @pl.when(level < levels - 1)
        def _():
            k_copy(c).wait_recv()

        first = k_in[c]
        second = advance(c, 2, first)

        @pl.when(level > 0)
        def _():
            k_out[c] = advance(c, 3, second)
            k_copy(c).start()

        outputs(c, 1, 2, first)
        outputs(c, 1, 3, second)
        y_copy(c, 1).start()

    lag = 2 * (levels - level) - 1

    @pl.loop(0, count + 2 * levels - 1)
    def _(t):
        @pl.when(t < count)
        def _():
            forward(t)

        @pl.when(jnp.logical_and(t >= lag, t < lag + count))
        def _():
            backward(t - lag)

    for copy in smalls:
        copy.wait_send()

    @pl.loop(0, count)
    def _(c):
        x_copy(c).wait_send()

        @pl.when(level < levels - 1)
        def _():
            f_copy(c).wait_send()

        @pl.when(level > 0)
        def _():
            k_copy(c).wait_send()

        for k in range(2):
            y_copy(c, k).wait_send()
            y_landed(c, k).wait_recv()


def on_device(features, log_decay, step_size, b_matrix, c_matrix, skip_gain):
    heads, rows = log_decay.shape
    lanes = features.shape[1]
    width = lanes // heads
    groups = b_matrix.shape[1] // N
    per_group = heads // groups
    units = heads // UNIT
    n = lax.axis_size("ctx")

    upto = (jnp.arange(SPAN)[:, None] <= jnp.arange(SPAN)[None, :]).astype(F32)
    cumulative = jnp.einsum(
        "hks,st->hkt", log_decay.reshape(heads, 2, SPAN), upto, precision=lax.Precision.HIGHEST
    )
    ends = cumulative[:, :, -1]
    coeffs = jnp.exp(ends[:, :, None] - cumulative).reshape(heads, rows) * step_size
    cumulative = cumulative.reshape(heads, rows)
    cum_rows = cumulative.reshape(units, UNIT, rows)
    step_rows = step_size.reshape(units, UNIT, rows)
    cum_cols = jnp.swapaxes(cum_rows, 1, 2)
    coeff_cols = jnp.swapaxes(coeffs.reshape(units, UNIT, rows), 1, 2)
    skip_row = jnp.repeat(skip_gain, width)[None, :]
    decay = jnp.repeat(jnp.exp(ends).T, width, axis=1)
    decay = jnp.concatenate([decay, jnp.zeros((6, lanes), F32)], axis=0)

    wide = pl.BlockSpec((rows, UNIT * width), lambda j: (0, j))
    tall = pl.BlockSpec((1, rows, UNIT), lambda j: (j, 0, 0))
    flat = pl.BlockSpec((1, UNIT, rows), lambda j: (j, 0, 0))
    grouped = pl.BlockSpec((rows, N), lambda j: (0, j * UNIT // per_group))
    line = pl.BlockSpec((1, UNIT * width), lambda j: (0, j))

    weighted = pl.pallas_call(
        functools.partial(scale_kernel, width),
        grid=(units,),
        out_shape=jax.ShapeDtypeStruct((rows, lanes), F32),
        in_specs=[wide, tall],
        out_specs=wide,
    )(features, coeff_cols)

    half = lanes // 2
    chunk = min(256, half)
    count = half // chunk
    held = max(1, groups // 2)
    vmem = pl.BlockSpec(memory_space=pltpu.VMEM)
    dma = lambda k: pltpu.SemaphoreType.DMA((k,))
    state = pltpu.VMEM((count, N, chunk), F32)
    state_part = pl.pallas_call(
        functools.partial(chain_kernel, n, chunk, per_group * width),
        out_shape=jax.ShapeDtypeStruct((rows, lanes), F32),
        in_specs=[vmem] * 4,
        out_specs=vmem,
        scratch_shapes=[
            pltpu.VMEM((held * N, rows), F32),
            pltpu.VMEM((rows, held * N), F32),
            pltpu.VMEM((8, half), F32),
            pltpu.VMEM((count, rows, chunk), F32),
            pltpu.VMEM((4, held * N, SPAN), BF),
            pltpu.VMEM((4, SPAN, held * N), BF),
            pltpu.VMEM((4, 8, half), F32),
            pltpu.VMEM((count, 4, N, chunk), F32),
            state, state, state, state,
            pltpu.VMEM((2, count, SPAN, chunk), F32),
            dma(3), dma(3),
        ] + [dma(count)] * 10,
        compiler_params=pltpu.CompilerParams(
            collective_id=0, has_side_effects=True, vmem_limit_bytes=LIMIT
        ),
    )(weighted, b_matrix.T.astype(F32), c_matrix.astype(F32), decay)

    return pl.pallas_call(
        functools.partial(mix_kernel, width),
        grid=(units,),
        out_shape=jax.ShapeDtypeStruct((rows, lanes), BF),
        in_specs=[wide, tall, flat, flat, grouped, grouped, line, wide],
        out_specs=wide,
    )(features, cum_cols, cum_rows, step_rows, b_matrix, c_matrix, skip_row, state_part)


def solution(mesh):
    placed = (
        P("ctx", "head"),
        P("head", "ctx"),
        P("head", "ctx"),
        P("ctx", "head"),
        P("ctx", "head"),
        P("head"),
    )
    return jax.shard_map(
        on_device, mesh=mesh, in_specs=placed, out_specs=P("ctx", "head"), check_vma=False
    )
```

profile of v0, /device:TPU:0, one launch (start us, length us, event | category | flops | bytes accessed | tf_op | source)
XLA Modules:
  0.0 156.3 jit_solution(4966888476787859700)
XLA Ops:
  0.0 0.0 copy-start
  0.0 0.8 copy-done
  0.8 0.2 convolution_bitcast_fusion
  1.0 0.2 slice_reduce_fusion
  1.2 0.9 fusion
  2.1 0.0 copy-start.2
  2.1 1.3 copy.14
  3.5 0.0 copy-start.1
  3.5 7.5 %shard_map.64.wt = f32[256,4096]{1,0:T(8,128)} custom-call(bf16[256,4096]{1,0:T(8,128)(2,1)} %x_ref.3, f32[8,256,8]{2,1,0:T(8,128)} %bitcast.28), custom_call_target="tpu_custom_call" | custom-call | tf_op jit(solution)/shard_map/pallas_call | solution.py:264
  10.9 0.1 broadcast_in_dim.10
  11.0 0.1 reshape.19
  11.1 0.7 concatenate.3.dec
  11.8 0.0 copy-done.2
  11.8 0.1 copy.15
  11.9 0.8 convert_bitcast_fusion.bt
  12.8 0.0 copy-done.1
  12.8 0.9 convert_element_type.11.cc
  13.7 0.0 copy-start.4
  13.7 119.0 %shard_map.65.sp_ref = f32[256,4096]{1,0:T(8,128)} custom-call(f32[256,4096]{1,0:T(8,128)} %shard_map.64.wt, f32[512,256]{1,0:T(8,128)} %convert_bitcast_fusion.bt, f32[256,512]{1,0:T(8,128)} %convert_element_type.11.cc, f32[8,4096]{1,0:T(8,128)} %concatenate.3.dec), custom_call_target="tpu_custom_call" | custom-call | tf_op jit(solution)/shard_map/pallas_call | solution.py:279
  132.7 0.1 copy.12
  132.8 0.1 reshape_reshape.3.cr_ref
  132.8 0.0 copy-start.3
  132.8 1.3 copy.16.ct_ref
  134.2 0.0 copy-done.4
  134.2 0.1 broadcast_in_dim.4
  134.2 0.7 broadcast_in_dim_reshape.3.skip_ref
  134.9 0.0 copy-done.3
  134.9 21.4 %shard_map.66 = bf16[256,4096]{1,0:T(8,128)(2,1)} custom-call(bf16[256,4096]{1,0:T(8,128)(2,1)} %x_ref.3, f32[8,256,8]{2,1,0:T(8,128)} %copy.16.ct_ref, f32[8,8,256]{2,1,0:T(8,128)} %copy-done.3, f32[8,8,256]{2,1,0:T(8,128)} %bitcast.30, bf16[256,512]{1,0:T(8,128)(2,1)} %b_ref.1, bf16[256,512]{1,0:T(8,128)(2,1)} %c_ref.1, ...), custom_call_target="tpu_custom_call" | custom-call | tf_op jit(solution)/shard_map/pallas_call | solution.py:302
  (1 shorter events, 0.0 us)
Async XLA Ops:
  0.0 0.8 copy-start
  2.1 9.6 %copy-start.2 = (bf16[256,512]{1,0:T(8,128)(2,1)S(1)}, bf16[256,512]{1,0:T(8,128)(2,1)}, u32[]{:S(2)}) copy-start(bf16[256,512]{1,0:T(8,128)(2,1)} %b_ref.1) | copy-start | bytes 786436
  3.5 9.3 %copy-start.1 = (bf16[256,512]{1,0:T(8,128)(2,1)S(1)}, bf16[256,512]{1,0:T(8,128)(2,1)}, u32[]{:S(2)}) copy-start(bf16[256,512]{1,0:T(8,128)(2,1)} %c_ref.1) | copy-start | bytes 786436
  13.7 120.5 %copy-start.4 = (f32[64]{0:T(128)S(1)}, f32[64]{0:T(128)}, u32[]{:S(2)}) copy-start(f32[64]{0:T(128)} %param.11) | copy-start | bytes 772
  132.8 2.1 %copy-start.3 = (f32[8,8,256]{2,1,0:T(8,128)}, f32[8,8,256]{2,1,0:T(8,128)S(1)}, u32[]{:S(2)}) copy-start(f32[8,8,256]{2,1,0:T(8,128)S(1)} %reshape_reshape.3.cr_ref) | copy-start | bytes 196612
where the time goes:
time: 157 us; the launch traced here: 156 us
  Pallas kernels  148 us (94%)
  local copies, waits for them, and re-layouts  5.5 us (4%)
  other arithmetic  2.67 us (2%)
    pallas_call x1, Pallas kernels, on_device(): pl.pallas_call(functools.partial(chain_kernel, n, chunk, per_group * widt...  119 us
    pallas_call x1, Pallas kernels, on_device(): pl.pallas_call(functools.partial(mix_kernel, width), grid=(units,), out_s...  21.4 us
    pallas_call x1, Pallas kernels, on_device(): pl.pallas_call(functools.partial(scale_kernel, width), grid=(units,), out...  7.47 us

commit v1 on v0

v1 whole, which is shorter than its diff:
```python
import functools

import jax
import jax.numpy as jnp
from jax import lax
from jax.experimental import pallas as pl
from jax.experimental.pallas import tpu as pltpu
from jax.sharding import PartitionSpec as P

N = 256
SPAN = 128
UNIT = 4
REST = 3
MESH = pl.DeviceIdType.MESH
LIMIT = 56 * 1024 * 1024
BF = jnp.bfloat16
F32 = jnp.float32


def spread(values, width):
    rows = values.shape[0]
    return jnp.concatenate(
        [jnp.broadcast_to(values[:, h : h + 1], (rows, width)) for h in range(UNIT)], axis=1
    )


def layer_kernel(
    n, per_group, width, x_ref, cols_ref, rows_ref, step_ref, b_ref, c_ref, skip_ref, o_ref,
    b_out, c_out, d_out, x_out, b_in, c_in, d_in, x_in, b_slot, c_slot, d_slot, scores, acc,
    states, f_out, f_in, k_out, k_in, y_out, y_in,
    small_s, small_r, x_s, x_r, f_s, f_r, k_s, k_r, yf_s, yf_r, yk_s, yk_r,
):
    me = lax.axis_index("ctx")
    level, side = me // 2, lax.rem(me, 2)
    levels = n // 2
    partner = me + 1 - 2 * side
    after, before = lax.rem(me + 2, n), lax.rem(me + n - 2, n)
    chunk = UNIT * width
    count = d_in.shape[1] // chunk
    groups = b_ref.shape[1] // N
    held = b_in.shape[1] // N
    mine, other = side * count, (1 - side) * count
    g_mine, g_other = (side * groups) // 2 * N, ((1 - side) * groups) // 2 * N

    def remote(src, dst, send, recv, device):
        return pltpu.make_async_remote_copy(
            src_ref=src, dst_ref=dst, send_sem=send, recv_sem=recv,
            device_id={"ctx": device}, device_id_type=MESH,
        )

    def at(start, length):
        return pl.ds(pl.multiple_of(start, 128), length)

    def lanes(unit):
        return at(unit * chunk, chunk)

    def toks(k):
        return slice(k * SPAN, (k + 1) * SPAN)

    b_copy = remote(b_out, b_in, small_s.at[0], small_r.at[0], partner)
    c_copy = remote(c_out, c_in, small_s.at[1], small_r.at[1], partner)
    d_copy = remote(d_out, d_in, small_s.at[2], small_r.at[2], partner)

    def x_copy(c):
        return remote(x_out.at[c], x_in.at[c], x_s.at[c], x_r.at[c], partner)

    def f_copy(c):
        return remote(f_out.at[c], f_in.at[c], f_s.at[c], f_r.at[c], after)

    def k_copy(c):
        return remote(k_out.at[c], k_in.at[c], k_s.at[c], k_r.at[c], before)

    def y_copy(c, k):
        send, recv = (yf_s, yf_r) if k == 0 else (yk_s, yk_r)
        return remote(y_out.at[k, c], y_in.at[k, c], send.at[c], recv.at[c], partner)

    def weighted(unit):
        coeffs = spread(cols_ref[unit, :, UNIT : 2 * UNIT], width)
        return (x_ref[:, lanes(unit)].astype(F32) * coeffs).astype(BF)

    def decays(unit):
        ends = [
            jnp.exp(cols_ref[unit, (k + 1) * SPAN - 8 : (k + 1) * SPAN, 0:UNIT])[7:8] for k in range(2)
        ]
        front, back = (jnp.broadcast_to(spread(e, width), (8, chunk)) for e in ends)
        return jnp.where(lax.broadcasted_iota(jnp.int32, (8, chunk), 0) < 4, front, back)

    def send_x(c):
        x_out[c] = weighted(other + c).astype(F32)
        x_copy(c).start()

    barrier = pltpu.get_barrier_semaphore()
    for device in (partner, after, before):
        pl.semaphore_signal(barrier, inc=1, device_id={"ctx": device}, device_id_type=MESH)
    b_out[...] = b_ref[:, at(g_other, held * N)].astype(F32)
    c_out[...] = c_ref[:, at(g_other, held * N)].astype(F32)
    pl.semaphore_wait(barrier, 3)
    b_copy.start()
    send_x(0)

    @pl.loop(0, count)
    def _(c):
        d_out[:, lanes(c)] = decays(other + c)

    d_copy.start()
    c_copy.start()

    @pl.loop(1, count)
    def _(c):
        send_x(c)

    here = (side, 3 - side)
    there = (1 - side, 2 + side)
    for k in range(2):
        b_slot[here[k]] = b_ref[toks(k), at(g_mine, held * N)].astype(F32).T.astype(BF)
        c_slot[here[k]] = c_ref[toks(k), at(g_mine, held * N)]
        for g in range(groups):
            part = slice(g * N, (g + 1) * N)
            scores[k * groups + g] = lax.dot_general(
                c_ref[toks(k), part], b_ref[toks(k), part], (((1,), (1,)), ((), ())),
                preferred_element_type=F32,
            )

    @pl.loop(0, count)
    def _(c):
        both = decays(mine + c)
        d_slot[here[0], :, lanes(c)] = jnp.broadcast_to(both[0:1], (8, chunk))
        d_slot[here[1], :, lanes(c)] = jnp.broadcast_to(both[4:5], (8, chunk))

    row = lax.broadcasted_iota(jnp.int32, (SPAN, SPAN), 0)
    col = lax.broadcasted_iota(jnp.int32, (SPAN, SPAN), 1)

    def diagonal(unit):
        group = (unit * UNIT) // per_group
        for k in range(2):
            grouped = scores[k * groups + group]
            x = x_ref[toks(k), lanes(unit)]
            parts = []
            for h in range(UNIT):
                down = cols_ref[unit, toks(k), h : h + 1]
                gaps = jnp.where(row >= col, down - rows_ref[unit, h : h + 1, toks(k)], -jnp.inf)
                weights = (grouped * jnp.exp(gaps) * step_ref[unit, h : h + 1, toks(k)]).astype(BF)
                own = x[:, h * width : (h + 1) * width]
                part = jnp.dot(weights, own, preferred_element_type=F32)
                parts.append(part + skip_ref[unit * UNIT + h] * own.astype(F32))
            acc[toks(k), lanes(unit)] = jnp.concatenate(parts, axis=1)

    def finish(unit, k, y):
        scale = spread(jnp.exp(cols_ref[unit, toks(k), 0:UNIT]), width)
        o_ref[toks(k), lanes(unit)] = (acc[toks(k), lanes(unit)] + y * scale).astype(BF)

    @pl.loop(0, count)
    def _(c):
        diagonal(mine + c)

    b_copy.wait_recv()
    d_copy.wait_recv()
    for k in range(2):
        b_slot[there[k]] = b_in[toks(k), :].T.astype(BF)
        d_slot[there[k]] = jnp.broadcast_to(d_in[4 * k : 4 * k + 1, :], d_in.shape)
    c_copy.wait_recv()
    for k in range(2):
        c_slot[there[k]] = c_in[toks(k), :].astype(BF)

    def group_rows(c):
        return at((c * UNIT) // per_group * N, N)

    def outputs(c, k, first, second):
        early = jnp.dot(c_slot[2 * k, :, group_rows(c)], first.astype(BF), preferred_element_type=F32)
        late = jnp.dot(
            c_slot[2 * k + 1, :, group_rows(c)], second.astype(BF), preferred_element_type=F32
        )
        is_early = here[k] == 2 * k
        y_out[k, c] = jnp.where(is_early, late, early)
        y_copy(c, k).start()
        finish(mine + c, k, jnp.where(is_early, early, late))

    def advance(c, slot, entering):
        return d_slot[slot, 0:1, lanes(c)] * entering + states[c, slot]

    def forward(c):
        own = weighted(mine + c)
        for k in range(2):
            states[c, here[k]] = jnp.dot(
                b_slot[here[k], group_rows(c), :], own[toks(k)], preferred_element_type=F32
            )
        x_copy(c).wait_recv()
        for k in range(2):
            states[c, there[k]] = jnp.dot(
                b_slot[there[k], group_rows(c), :], x_in[c, toks(k), :].astype(BF),
                preferred_element_type=F32,
            )

        @pl.when(level == 0)
        def _():
            f_in[c] = jnp.zeros(f_in.shape[1:], F32)

        @pl.when(level > 0)
        def _():
            f_copy(c).wait_recv()

        first = f_in[c]
        second = advance(c, 0, first)
        last = advance(c, 1, second)

        @pl.when(level < levels - 1)
        def _():
            f_out[c] = last
            f_copy(c).start()

        @pl.when(level == levels - 1)
        def _():
            k_in[c] = last

        outputs(c, 0, first, second)

    def backward(c):
        @pl.when(level < levels - 1)
        def _():
            k_copy(c).wait_recv()

        first = k_in[c]
        second = advance(c, 2, first)

        @pl.when(level > 0)
        def _():
            k_out[c] = advance(c, 3, second)
            k_copy(c).start()

        outputs(c, 1, first, second)

    lag = 2 * (levels - level) - 1

    @pl.loop(0, count + 2 * levels - 1 + REST)
    def _(t):
        @pl.when(t < count)
        def _():
            forward(t)

        @pl.when(jnp.logical_and(t >= lag, t < lag + count))
        def _():
            backward(t - lag)

        @pl.when(t < count)
        def _():
            diagonal(other + t)

        @pl.when(jnp.logical_and(t >= lag + REST, t < lag + REST + count))
        def _():
            c = t - lag - REST
            for k in range(2):
                y_copy(c, k).wait_recv()
                finish(other + c, k, y_in[k, c])

    for copy in (b_copy, c_copy, d_copy):
        copy.wait_send()

    @pl.loop(0, count)
    def _(c):
        x_copy(c).wait_send()

        @pl.when(level < levels - 1)
        def _():
            f_copy(c).wait_send()

        @pl.when(level > 0)
        def _():
            k_copy(c).wait_send()

        for k in range(2):
            y_copy(c, k).wait_send()


def on_device(features, log_decay, step_size, b_matrix, c_matrix, skip_gain):
    heads, rows = log_decay.shape
    lanes = features.shape[1]
    width = lanes // heads
    groups = b_matrix.shape[1] // N
    per_group = heads // groups
    units = heads // UNIT
    n = lax.axis_size("ctx")

    upto = (jnp.arange(SPAN)[:, None] <= jnp.arange(SPAN)[None, :]).astype(F32)
    cumulative = jnp.einsum(
        "hks,st->hkt", log_decay.reshape(heads, 2, SPAN), upto, precision=lax.Precision.HIGHEST
    )
    ends = cumulative[:, :, -1]
    coeffs = jnp.exp(ends[:, :, None] - cumulative).reshape(heads, rows) * step_size
    cum_rows = cumulative.reshape(units, UNIT, rows)
    step_rows = step_size.reshape(units, UNIT, rows)
    columns = jnp.concatenate([cum_rows, coeffs.reshape(units, UNIT, rows)], axis=1)
    columns = jnp.swapaxes(columns, 1, 2)

    half = lanes // 2
    chunk = UNIT * width
    count = half // chunk
    held = max(1, groups // 2)
    vmem = pl.BlockSpec(memory_space=pltpu.VMEM)
    smem = pl.BlockSpec(memory_space=pltpu.SMEM)
    dma = lambda k: pltpu.SemaphoreType.DMA((k,))
    wide = pltpu.VMEM((rows, held * N), F32)
    line = pltpu.VMEM((8, half), F32)
    block = pltpu.VMEM((count, rows, chunk), F32)
    state = pltpu.VMEM((count, N, chunk), F32)
    part = pltpu.VMEM((2, count, SPAN, chunk), F32)
    return pl.pallas_call(
        functools.partial(layer_kernel, n, per_group, width),
        out_shape=jax.ShapeDtypeStruct((rows, lanes), BF),
        in_specs=[vmem] * 6 + [smem],
        out_specs=vmem,
        scratch_shapes=[
            wide, wide, line, block,
            wide, wide, line, block,
            pltpu.VMEM((4, held * N, SPAN), BF),
            pltpu.VMEM((4, SPAN, held * N), BF),
            pltpu.VMEM((4, 8, half), F32),
            pltpu.VMEM((2 * groups, SPAN, SPAN), F32),
            pltpu.VMEM((rows, lanes), F32),
            pltpu.VMEM((count, 4, N, chunk), F32),
            state, state, state, state,
            part, part,
            dma(3), dma(3),
        ] + [dma(count)] * 10,
        compiler_params=pltpu.CompilerParams(
            collective_id=0, has_side_effects=True, vmem_limit_bytes=LIMIT
        ),
    )(features, columns, cum_rows, step_rows, b_matrix, c_matrix, skip_gain)


def solution(mesh):
    placed = (
        P("ctx", "head"),
        P("head", "ctx"),
        P("head", "ctx"),
        P("ctx", "head"),
        P("ctx", "head"),
        P("head"),
    )
    return jax.shard_map(
        on_device, mesh=mesh, in_specs=placed, out_specs=P("ctx", "head"), check_vma=False
    )
```

time: 157 us -> 130 us (0.83)
  Pallas kernels: 148 us -> 121 us
  local copies, waits for them, and re-layouts: 5.5 us -> 7.68 us
  other arithmetic: 2.67 us -> 0.97 us
    pallas_call x3 -> x1, Pallas kernels: 148 us -> 121 us  [on_device(): pl.pallas_call(functools.partial(layer_kernel, n, per_group, width), out_...]
    unnamed x11 -> x5, local copies, waits for them, and re-layouts: 0.99 us -> 3.97 us
    convert_element_type x2 -> x0, other arithmetic: 1.74 us -> none  [the longest x1 0.91 us: on_device(): c_matrix.astype(F32)]
where the time goes in v1:
time: 130 us
  Pallas kernels  121 us (93%)
  local copies, waits for them, and re-layouts  7.68 us (6%)
    pallas_call x1, Pallas kernels, on_device(): pl.pallas_call(functools.partial(layer_kernel, n, per_group, width), out_...  121 us
    unnamed x5, local copies, waits for them, and re-layouts  3.97 us

profile of v1, /device:TPU:0, one launch (start us, length us, event | category | flops | bytes accessed | tf_op | source)
XLA Modules:
  0.0 129.9 jit_solution(6191228199995221581)
XLA Ops:
  0.0 0.0 copy-start
  0.0 0.8 copy-done
  0.8 0.2 convolution_bitcast_fusion
  1.0 0.2 slice_reduce_fusion
  1.2 0.9 bitcast_multiply_fusion
  2.1 0.1 copy.11
  2.2 0.1 reshape.16.rows_ref
  2.3 0.0 copy-start.1
  2.3 1.5 %reshape.19.step_ref = f32[16,4,256]{2,1,0:T(4,128)} reshape(f32[64,256]{1,0:T(8,128)} %param.8) | data formatting | bytes 131072 | tf_op jit(solution)/shard_map/reshape | solution.py:290
  3.8 1.9 %copy.13.cols_ref = f32[16,256,8]{2,1,0:T(8,128)} copy(f32[16,256,8]{1,2,0:T(8,128)S(1)} %maximum_bitcast_fusion) | data formatting | bytes 262144 | tf_op jit(solution)/shard_map/transpose | solution.py:292
  5.7 0.0 copy-done.1
  5.8 121.0 %shard_map.64 = bf16[256,4096]{1,0:T(8,128)(2,1)} custom-call(bf16[256,4096]{1,0:T(8,128)(2,1)} %x_ref.1, f32[16,256,8]{2,1,0:T(8,128)} %copy.13.cols_ref, f32[16,4,256]{2,1,0:T(4,128)} %copy-done.1, f32[16,4,256]{2,1,0:T(4,128)} %reshape.19.step_ref, bf16[256,512]{1,0:T(8,128)(2,1)} %b_ref.1, bf16[256,512]{1,0:T(8,128)(2,1)} %c_ref.1, f32[64]{0:T(128)} %skip_ref.1), custom_call_target="tpu_custom_call" | custom-call | tf_op jit(solution)/shard_map/pallas_call | solution.py:306
  126.8 3.1 %copy.22 = bf16[256,4096]{1,0:T(8,128)(2,1)} copy(bf16[256,4096]{1,0:T(8,128)(2,1)} %shard_map.64) | data formatting | bytes 4194304
  (2 shorter events, 0.1 us)
Async XLA Ops:
  0.0 0.8 copy-start
  2.3 3.5 %copy-start.1 = (f32[16,4,256]{2,1,0:T(4,128)}, f32[16,4,256]{2,1,0:T(4,128)S(1)}, u32[]{:S(2)}) copy-start(f32[16,4,256]{2,1,0:T(4,128)S(1)} %reshape.16.rows_ref) | copy-start | bytes 196612

commit v2 on v1

--- a/solution.py
+++ b/solution.py
@@ -25,10 +25,10 @@
 
 
 def layer_kernel(
-    n, per_group, width, x_ref, cols_ref, rows_ref, step_ref, b_ref, c_ref, skip_ref, o_ref,
+    n, per_group, width, x_ref, decay_ref, step_ref, b_ref, c_ref, skip_ref, o_ref, cols_ref, rows_ref,
     b_out, c_out, d_out, x_out, b_in, c_in, d_in, x_in, b_slot, c_slot, d_slot, scores, acc,
     states, f_out, f_in, k_out, k_in, y_out, y_in,
-    small_s, small_r, x_s, x_r, f_s, f_r, k_s, k_r, yf_s, yf_r, yk_s, yk_r,
+    small_s, small_r, xf_s, xf_r, xk_s, xk_r, f_s, f_r, k_s, k_r, yf_s, yf_r, yk_s, yk_r,
 ):
     me = lax.axis_index("ctx")
     level, side = me // 2, lax.rem(me, 2)
@@ -61,8 +61,13 @@
     c_copy = remote(c_out, c_in, small_s.at[1], small_r.at[1], partner)
     d_copy = remote(d_out, d_in, small_s.at[2], small_r.at[2], partner)
 
-    def x_copy(c):
-        return remote(x_out.at[c], x_in.at[c], x_s.at[c], x_r.at[c], partner)
+    ends_here = level == 0
+    sends_less = jnp.logical_and(ends_here, side == 0)
+    gets_less = jnp.logical_and(ends_here, side == 1)
+
+    def x_copy(c, k):
+        send, recv = (xf_s, xf_r) if k == 0 else (xk_s, xk_r)
+        return remote(x_out.at[k, c], x_in.at[k, c], send.at[c], recv.at[c], partner)
 
     def f_copy(c):
         return remote(f_out.at[c], f_in.at[c], f_s.at[c], f_r.at[c], after)
@@ -86,12 +91,31 @@
         return jnp.where(lax.broadcasted_iota(jnp.int32, (8, chunk), 0) < 4, front, back)
 
     def send_x(c):
-        x_out[c] = weighted(other + c).astype(F32)
-        x_copy(c).start()
+        ready = weighted(other + c).astype(F32)
+        x_out[0, c] = ready[toks(0)]
+        x_copy(c, 0).start()
+
+        @pl.when(jnp.logical_not(sends_less))
+        def _():
+            x_out[1, c] = ready[toks(1)]
+            x_copy(c, 1).start()
 
     barrier = pltpu.get_barrier_semaphore()
     for device in (partner, after, before):
         pl.semaphore_signal(barrier, inc=1, device_id={"ctx": device}, device_id_type=MESH)
+    row = lax.broadcasted_iota(jnp.int32, (SPAN, SPAN), 0)
+    col = lax.broadcasted_iota(jnp.int32, (SPAN, SPAN), 1)
+    upto = (row <= col).astype(F32)
+    for k in range(2):
+        sums = jnp.dot(
+            decay_ref[:, toks(k)], upto, precision=lax.Precision.HIGHEST, preferred_element_type=F32
+        )
+        coeffs = jnp.exp(sums[:, SPAN - 1 :] - sums) * step_ref[:, toks(k)]
+        down, scale = sums.T, coeffs.T
+        for u in range(cols_ref.shape[0]):
+            own = slice(u * UNIT, (u + 1) * UNIT)
+            rows_ref[u, :, toks(k)] = jnp.concatenate([sums[own], step_ref[own, toks(k)]], axis=0)
+            cols_ref[u, toks(k), :] = jnp.concatenate([down[:, own], scale[:, own]], axis=1)
     b_out[...] = b_ref[:, at(g_other, held * N)].astype(F32)
     c_out[...] = c_ref[:, at(g_other, held * N)].astype(F32)
     pl.semaphore_wait(barrier, 3)
@@ -127,9 +151,6 @@
         d_slot[here[0], :, lanes(c)] = jnp.broadcast_to(both[0:1], (8, chunk))
         d_slot[here[1], :, lanes(c)] = jnp.broadcast_to(both[4:5], (8, chunk))
 
-    row = lax.broadcasted_iota(jnp.int32, (SPAN, SPAN), 0)
-    col = lax.broadcasted_iota(jnp.int32, (SPAN, SPAN), 1)
-
     def diagonal(unit):
         group = (unit * UNIT) // per_group
         for k in range(2):
@@ -139,7 +160,7 @@
             for h in range(UNIT):
                 down = cols_ref[unit, toks(k), h : h + 1]
                 gaps = jnp.where(row >= col, down - rows_ref[unit, h : h + 1, toks(k)], -jnp.inf)
-                weights = (grouped * jnp.exp(gaps) * step_ref[unit, h : h + 1, toks(k)]).astype(BF)
+                weights = (grouped * jnp.exp(gaps) * rows_ref[unit, UNIT + h : UNIT + h + 1, toks(k)]).astype(BF)
                 own = x[:, h * width : (h + 1) * width]
                 part = jnp.dot(weights, own, preferred_element_type=F32)
                 parts.append(part + skip_ref[unit * UNIT + h] * own.astype(F32))
@@ -172,7 +193,11 @@
         )
         is_early = here[k] == 2 * k
         y_out[k, c] = jnp.where(is_early, late, early)
-        y_copy(c, k).start()
+
+        @pl.when(jnp.logical_not(jnp.logical_and(gets_less, k == 0)))
+        def _():
+            y_copy(c, k).start()
+
         finish(mine + c, k, jnp.where(is_early, early, late))
 
     def advance(c, slot, entering):
@@ -184,12 +209,10 @@
             states[c, here[k]] = jnp.dot(
                 b_slot[here[k], group_rows(c), :], own[toks(k)], preferred_element_type=F32
             )
-        x_copy(c).wait_recv()
-        for k in range(2):
-            states[c, there[k]] = jnp.dot(
-                b_slot[there[k], group_rows(c), :], x_in[c, toks(k), :].astype(BF),
-                preferred_element_type=F32,
-            )
+        x_copy(c, 0).wait_recv()
+        states[c, there[0]] = jnp.dot(
+            b_slot[there[0], group_rows(c), :], x_in[0, c].astype(BF), preferred_element_type=F32
+        )
 
         @pl.when(level == 0)
         def _():
@@ -214,6 +237,13 @@
 
         outputs(c, 0, first, second)
 
+        @pl.when(jnp.logical_not(gets_less))
+        def _():
+            x_copy(c, 1).wait_recv()
+            states[c, there[1]] = jnp.dot(
+                b_slot[there[1], group_rows(c), :], x_in[1, c].astype(BF), preferred_element_type=F32
+            )
+
     def backward(c):
         @pl.when(level < levels - 1)
         def _():
@@ -248,8 +278,17 @@
         @pl.when(jnp.logical_and(t >= lag + REST, t < lag + REST + count))
         def _():
             c = t - lag - REST
+
+            @pl.when(sends_less)
+            def _():
+                y_in[0, c] = jnp.zeros(y_in.shape[2:], F32)
+
+            @pl.when(jnp.logical_not(sends_less))
+            def _():
+                y_copy(c, 0).wait_recv()
+
+            y_copy(c, 1).wait_recv()
             for k in range(2):
-                y_copy(c, k).wait_recv()
                 finish(other + c, k, y_in[k, c])
 
     for copy in (b_copy, c_copy, d_copy):
@@ -257,7 +296,16 @@
 
     @pl.loop(0, count)
     def _(c):
-        x_copy(c).wait_send()
+        x_copy(c, 0).wait_send()
+        y_copy(c, 1).wait_send()
+
+        @pl.when(jnp.logical_not(sends_less))
+        def _():
+            x_copy(c, 1).wait_send()
+
+        @pl.when(jnp.logical_not(gets_less))
+        def _():
+            y_copy(c, 0).wait_send()
 
         @pl.when(level < levels - 1)
         def _():
@@ -266,9 +314,6 @@
         @pl.when(level > 0)
         def _():
             k_copy(c).wait_send()
-
-        for k in range(2):
-            y_copy(c, k).wait_send()
 
 
 def on_device(features, log_decay, step_size, b_matrix, c_matrix, skip_gain):
@@ -279,17 +324,6 @@
     per_group = heads // groups
     units = heads // UNIT
     n = lax.axis_size("ctx")
-
-    upto = (jnp.arange(SPAN)[:, None] <= jnp.arange(SPAN)[None, :]).astype(F32)
-    cumulative = jnp.einsum(
-        "hks,st->hkt", log_decay.reshape(heads, 2, SPAN), upto, precision=lax.Precision.HIGHEST
-    )
-    ends = cumulative[:, :, -1]
-    coeffs = jnp.exp(ends[:, :, None] - cumulative).reshape(heads, rows) * step_size
-    cum_rows = cumulative.reshape(units, UNIT, rows)
-    step_rows = step_size.reshape(units, UNIT, rows)
-    columns = jnp.concatenate([cum_rows, coeffs.reshape(units, UNIT, rows)], axis=1)
-    columns = jnp.swapaxes(columns, 1, 2)
 
     half = lanes // 2
     chunk = UNIT * width
@@ -300,17 +334,18 @@
     dma = lambda k: pltpu.SemaphoreType.DMA((k,))
     wide = pltpu.VMEM((rows, held * N), F32)
     line = pltpu.VMEM((8, half), F32)
-    block = pltpu.VMEM((count, rows, chunk), F32)
     state = pltpu.VMEM((count, N, chunk), F32)
     part = pltpu.VMEM((2, count, SPAN, chunk), F32)
     return pl.pallas_call(
         functools.partial(layer_kernel, n, per_group, width),
         out_shape=jax.ShapeDtypeStruct((rows, lanes), BF),
-        in_specs=[vmem] * 6 + [smem],
+        in_specs=[vmem] * 5 + [smem],
         out_specs=vmem,
         scratch_shapes=[
-            wide, wide, line, block,
-            wide, wide, line, block,
+            pltpu.VMEM((units, rows, 2 * UNIT), F32),
+            pltpu.VMEM((units, 2 * UNIT, rows), F32),
+            wide, wide, line, part,
+            wide, wide, line, part,
             pltpu.VMEM((4, held * N, SPAN), BF),
             pltpu.VMEM((4, SPAN, held * N), BF),
             pltpu.VMEM((4, 8, half), F32),
@@ -320,11 +355,11 @@
             state, state, state, state,
             part, part,
             dma(3), dma(3),
-        ] + [dma(count)] * 10,
+        ] + [dma(count)] * 12,
         compiler_params=pltpu.CompilerParams(
             collective_id=0, has_side_effects=True, vmem_limit_bytes=LIMIT
         ),
-    )(features, columns, cum_rows, step_rows, b_matrix, c_matrix, skip_gain)
+    )(features, log_decay, step_size, b_matrix, c_matrix, skip_gain)
 
 
 def solution(mesh):

time: 130 us -> 126 us (0.969)
  local copies, waits for them, and re-layouts: 7.68 us -> 3.13 us
  Pallas kernels: 121 us -> 123 us
    transpose x1 -> x0, local copies, waits for them, and re-layouts: 1.93 us -> none  [on_device(): columns = jnp.swapaxes(columns, 1, 2)]
    pallas_call x1, Pallas kernels: 121 us -> 123 us  [on_device(): pl.pallas_call(functools.partial(layer_kernel, n, per_group, width), out_...]
    reshape x3 -> x0, local copies, waits for them, and re-layouts: 1.56 us -> none  [the longest x1 1.47 us: on_device(): step_rows = step_size.reshape(units, UNIT, rows)]
    unnamed x5 -> x1, local copies, waits for them, and re-layouts: 3.97 us -> 3.13 us
where the time goes in v2:
time: 126 us
  Pallas kernels  123 us (98%)
  local copies, waits for them, and re-layouts  3.13 us (2%)
    pallas_call x1, Pallas kernels, on_device(): pl.pallas_call(functools.partial(layer_kernel, n, per_group, width), out_...  123 us
    unnamed x1, local copies, waits for them, and re-layouts  3.13 us

profile of v2, /device:TPU:0, one launch (start us, length us, event | category | flops | bytes accessed | tf_op | source)
XLA Modules:
  0.0 125.9 jit_solution(10515211500367630853)
XLA Ops:
  0.0 122.8 %shard_map.64 = bf16[256,4096]{1,0:T(8,128)(2,1)} custom-call(bf16[256,4096]{1,0:T(8,128)(2,1)} %x_ref.1, f32[64,256]{1,0:T(8,128)} %decay_ref.1, f32[64,256]{1,0:T(8,128)} %step_ref.1, bf16[256,512]{1,0:T(8,128)(2,1)} %b_ref.1, bf16[256,512]{1,0:T(8,128)(2,1)} %c_ref.1, f32[64]{0:T(128)} %skip_ref.1), custom_call_target="tpu_custom_call" | custom-call | tf_op jit(solution)/shard_map/pallas_call | solution.py:339
  122.8 3.1 %copy.8 = bf16[256,4096]{1,0:T(8,128)(2,1)} copy(bf16[256,4096]{1,0:T(8,128)(2,1)} %shard_map.64) | data formatting | bytes 4194304

commit v3 on v2

--- a/solution.py
+++ b/solution.py
@@ -10,7 +10,7 @@
 N = 256
 SPAN = 128
 UNIT = 4
-REST = 3
+REST = 5
 MESH = pl.DeviceIdType.MESH
 LIMIT = 56 * 1024 * 1024
 BF = jnp.bfloat16
@@ -94,11 +94,7 @@
         ready = weighted(other + c).astype(F32)
         x_out[0, c] = ready[toks(0)]
         x_copy(c, 0).start()
-
-        @pl.when(jnp.logical_not(sends_less))
-        def _():
-            x_out[1, c] = ready[toks(1)]
-            x_copy(c, 1).start()
+        x_out[1, c] = ready[toks(1)]
 
     barrier = pltpu.get_barrier_semaphore()
     for device in (partner, after, before):
@@ -133,6 +129,12 @@
     def _(c):
         send_x(c)
 
+    @pl.when(jnp.logical_not(sends_less))
+    def _():
+        @pl.loop(0, count)
+        def _(c):
+            x_copy(c, 1).start()
+
     here = (side, 3 - side)
     there = (1 - side, 2 + side)
     for k in range(2):
@@ -237,6 +239,7 @@
 
         outputs(c, 0, first, second)
 
+    def backward(c):
         @pl.when(jnp.logical_not(gets_less))
         def _():
             x_copy(c, 1).wait_recv()
@@ -244,7 +247,6 @@
                 b_slot[there[1], group_rows(c), :], x_in[1, c].astype(BF), preferred_element_type=F32
             )
 
-    def backward(c):
         @pl.when(level < levels - 1)
         def _():
             k_copy(c).wait_recv()

time: 126 us -> 122 us (0.968)
  Pallas kernels: 123 us -> 119 us
    pallas_call x1, Pallas kernels: 123 us -> 119 us  [on_device(): pl.pallas_call(functools.partial(layer_kernel, n, per_group, width), out_...]
where the time goes in v3:
time: 122 us
  Pallas kernels  119 us (98%)
  local copies, waits for them, and re-layouts  3.13 us (3%)
    pallas_call x1, Pallas kernels, on_device(): pl.pallas_call(functools.partial(layer_kernel, n, per_group, width), out_...  119 us
    unnamed x1, local copies, waits for them, and re-layouts  3.13 us

profile of v3, /device:TPU:0, one launch (start us, length us, event | category | flops | bytes accessed | tf_op | source)
XLA Modules:
  0.0 121.9 jit_solution(14843245624575747187)
XLA Ops:
  0.0 118.7 %shard_map.64 = bf16[256,4096]{1,0:T(8,128)(2,1)} custom-call(bf16[256,4096]{1,0:T(8,128)(2,1)} %x_ref.1, f32[64,256]{1,0:T(8,128)} %decay_ref.1, f32[64,256]{1,0:T(8,128)} %step_ref.1, bf16[256,512]{1,0:T(8,128)(2,1)} %b_ref.1, bf16[256,512]{1,0:T(8,128)(2,1)} %c_ref.1, f32[64]{0:T(128)} %skip_ref.1), custom_call_target="tpu_custom_call" | custom-call | tf_op jit(solution)/shard_map/pallas_call | solution.py:341
  118.7 3.1 %copy.8 = bf16[256,4096]{1,0:T(8,128)(2,1)} copy(bf16[256,4096]{1,0:T(8,128)(2,1)} %shard_map.64) | data formatting | bytes 4194304
